TPU v7x, 256 devices: a whole 4x4x8 slice. The times are simulated.
256 devices in a mesh: pts: 32 (over z_lo, y, core), ctr: 8 (over x, z_hi).
Axes of the slice: x: 4, y: 4, z: 8 (z_hi: 2, z_lo: 4; z = z_hi * 4 + z_lo), core: 2. Of those that a mesh axis runs over, the one named last changes fastest.
Arguments:
- points: float32 [90, 65536], P(None, 'pts'), may hold values from -6 to 6
- centre_index: int32 [65536], P(('ctr', 'pts')), may hold values from 0 to 65535, as said below
- inv_scale: float32 [90], replicated, may hold values from 0.08 to 0.3
- left_cols: bfloat16 [64, 65536], P(None, 'pts'), may hold values from -0.375 to 0.375
- right_cols: bfloat16 [64, 65536], P(None, ('ctr', 'pts')), may hold values from -0.375 to 0.375
Outputs:
- point_side: float32 [64, 65536], P(None, 'pts')
- centre_side: float32 [64, 65536], P(None, ('ctr', 'pts'))
Inputs may be any that keep to these rules, and one draw needn't show every extreme that they name: `centre_index`: indices of the centres among the 65536 sampled points; repeats may occur, and both 0 and 65535 are taken in every draw.
All inputs are finite; a program needn't handle non-finite values.
Results may differ from a plain program's by a relative error of at most 0.012.
Values may be sent and summed in bfloat16 or wider, within the bound.
A program may use at most 64 MiB of HBM per device.

v0:
```python
import math

import jax
import jax.numpy as jnp
from jax import lax
from jax.sharding import PartitionSpec as P


def tile_of(scaled_blk, norm_blk, scaled_ctr, norm_ctr):
    cross = lax.dot_general(
        scaled_blk, scaled_ctr, (((0,), (0,)), ((), ())), preferred_element_type=jnp.float32
    )
    dist = jnp.maximum(norm_blk[:, None] + norm_ctr[None, :] - 2.0 * cross, 0.0)
    return jnp.exp(-0.5 * dist).astype(jnp.bfloat16)


def body(points, centre_index, inv_scale, left_cols, right_cols):
    rows_here = points.shape[1]
    offset = lax.axis_index("pts") * rows_here
    indices = lax.all_gather(centre_index, "pts", axis=0, tiled=True)
    local_idx = indices - offset
    inside = (local_idx >= 0) & (local_idx < rows_here)
    taken_rows = jnp.take(points, jnp.clip(local_idx, 0, rows_here - 1), axis=1)
    picked = jnp.where(inside[None, :], taken_rows, 0.0)
    scale_col = inv_scale[:, None]
    centre_raw = lax.psum(picked, "pts")
    scaled_ctr = (centre_raw * scale_col).astype(jnp.bfloat16)
    panel_cols = lax.all_gather(right_cols, "pts", axis=1, tiled=True)
    norm_ctr = jnp.sum(jnp.square(scaled_ctr.astype(jnp.float32)), axis=0)
    scaled_pts = (points * scale_col).astype(jnp.bfloat16)
    norm_pts = jnp.sum(jnp.square(scaled_pts.astype(jnp.float32)), axis=0)
    width_rows = left_cols.shape[0]
    block_rows = math.gcd(rows_here, 512)
    count_blocks = rows_here // block_rows
    numbers = jnp.arange(count_blocks, dtype=jnp.int32)

    def kernel_at(number):
        start = number * block_rows
        scaled_blk = lax.dynamic_slice_in_dim(scaled_pts, start, block_rows, 1)
        norm_blk = lax.dynamic_slice_in_dim(norm_pts, start, block_rows, 0)
        left_blk = lax.dynamic_slice_in_dim(left_cols, start, block_rows, 1)
        return (tile_of(scaled_blk, norm_blk, scaled_ctr, norm_ctr), left_blk)

    def point_product(kernel_tile):
        return lax.dot_general(
            panel_cols, kernel_tile, (((1,), (1,)), ((), ())), preferred_element_type=jnp.float32
        )

    empty = jnp.zeros((width_rows, scaled_ctr.shape[1]), jnp.float32)

    def advance(running, number):
        kernel_tile, left_blk = kernel_at(number)
        running = running + jnp.dot(left_blk, kernel_tile, preferred_element_type=jnp.float32)
        return (running, point_product(kernel_tile))

    centre_part, point_blocks = lax.scan(advance, empty, numbers)
    point_part = jnp.transpose(point_blocks, (1, 0, 2)).reshape(width_rows, rows_here)
    point_side = lax.psum(point_part, "ctr")
    centre_side = lax.psum_scatter(centre_part, "pts", scatter_dimension=1, tiled=True)
    return (point_side, centre_side)


def solution(mesh):
    return jax.shard_map(
        body,
        mesh=mesh,
        in_specs=(P(None, "pts"), P(("ctr", "pts")), P(), P(None, "pts"), P(None, ("ctr", "pts"))),
        out_specs=(P(None, "pts"), P(None, ("ctr", "pts"))),
        check_vma=False,
    )
```

profile of v0, /device:TPU:4, one launch (start us, length us, event | category | flops | bytes accessed | tf_op | source)
XLA Modules:
  0.0 756.4 jit_solution(14805183272187710918)
XLA Ops:
  7.2 44.9 %all-gather = s32[32,1,256]{2,1,0:T(1,128)S(1)} all-gather(s32[1,1,256]{2,1,0:T(1,128)} %bitcast.34), channel_id=1, replica_groups=mesh['pts'=32,'ctr'=8] {'pts'}, dimensions={0}, use_global_device_ids=true | all-gather | bytes 33792 | tf_op jit(solution)/shard_map/all_gather | solution.py:20
  52.4 1.5 copy.13
  53.8 27.7 %gather_fusion = f32[8192,90]{1,0:T(8,128)} fusion(f32[90,2048]{0,1:T(8,128)S(1)} %copy.13, s32[8192]{0:T(1024)S(1)} %fusion.5), kind=kCustom, calls=%fused_computation | custom fusion | bytes 5931008 | tf_op jit(solution)/shard_map/jit(_take)/gather | solution.py:23
  81.6 7.6 %select_bitcast_fusion = f32[90,8192]{0,1:T(8,128)} fusion(f32[8192,90]{1,0:T(8,128)} %gather_fusion, pred[8192]{0:T(1024)(128)(4,1)S(1)} %reshape.39, pred[8192]{0:T(1024)(128)(4,1)S(1)} %compare_and_fusion), kind=kLoop, calls=%fused_computation.9 | loop fusion | flops 1474560 | bytes 5914624 | tf_op jit(solution)/shard_map/jit(_where)/select_n | solution.py:24
  89.3 0.7 all-gather.3.cloned.1.call-update
  90.4 0.9 multiply_reduce_fusion.1
  91.3 284.0 %all-reduce.3.cloned.1.call-done = f32[90,8192]{0,1:T(8,128)} async-done(((f32[90,8192]{0,1:T(8,128)}), f32[90,8192]{0,1:T(8,128)}) %all-reduce.3.cloned.1.call-update) | async-done | bytes 2949136 | tf_op jit(solution)/shard_map/psum | solution.py:26
  375.3 4.5 multiply_reduce_fusion
  379.9 3.9 copy.14
  383.8 53.1 %all-gather.3.cloned.1.call-done = bf16[64,8192]{1,0:T(8,128)(2,1)} async-done(((bf16[64,256]{1,0:T(8,128)(2,1)}), bf16[64,8192]{1,0:T(8,128)(2,1)}) %all-gather.3.cloned.1.call-update) | async-done | bytes 1048592 | tf_op jit(solution)/shard_map/all_gather | solution.py:28
  436.9 54.1 %while.13 = (s32[]{:T(128)}, f32[64,8192]{1,0:T(8,128)S(1)}, f32[4,64,512]{2,1,0:T(8,128)S(1)}, s32[4]{0:T(128)S(1)}, bf16[64,2048]{1,0:T(8,128)(2,1)}, /*index=...) while((s32[]{:T(128)}, f32[64,8192]{1,0:T(8,128)S(1)}, ...), condition=%wide.region_4.5_spmd.clone, body=%wide.region_3.4_spmd.clone.sunk | while | flops 1854930944 | bytes 36509948 | solution.py:56
  436.9 0.6 dynamic_slice.27
  438.2 6.8 exponential_convert_fusion.2
  445.0 2.7 fusion.23
  447.7 2.7 convolution_add_fusion.2
  450.4 0.6 dynamic_slice.27
  451.8 6.8 exponential_convert_fusion.2
  458.5 2.7 fusion.23
  461.2 2.7 convolution_add_fusion.2
  464.0 0.6 dynamic_slice.27
  465.3 6.8 exponential_convert_fusion.2
  472.1 2.7 fusion.23
  474.8 2.7 convolution_add_fusion.2
  477.5 0.6 dynamic_slice.27
  478.8 6.8 exponential_convert_fusion.2
  485.6 2.7 fusion.23
  488.3 2.7 convolution_add_fusion.2
  491.1 0.9 copy.16
  492.0 0.5 copy-done
  492.6 107.9 %all-reduce.5.cloned.1.call-done = f32[64,2048]{1,0:T(8,128)} async-done(((f32[64,2048]{1,0:T(8,128)}), f32[64,2048]{1,0:T(8,128)}) %all-reduce.5.cloned.1.call-update) | async-done | bytes 524304 | tf_op jit(solution)/shard_map/psum | solution.py:58
  600.5 147.5 %reduce-scatter.2.cloned.1.call-done = f32[64,256]{1,0:T(8,128)} async-done(((f32[64,8192]{1,0:T(8,128)}), f32[64,256]{1,0:T(8,128)}) %reduce-scatter.2.cloned.1.call-update) | async-done | bytes 65552 | tf_op jit(solution)/shard_map/reduce_scatter | solution.py:59
  748.0 1.9 copy.29
  (32 shorter events, 1.1 us)
Async XLA Ops:
  7.2 368.2 %all-reduce.3.cloned.1.call-start = ((), (), s32[]{:S(2)}) async-start(), calls=%async_computation.1 | async-start | bytes 8388608 | tf_op jit(solution)/shard_map/psum | solution.py:26
  89.2 1.1 copy-start.2
  89.2 1.1 copy-start.3
  89.3 347.6 %all-gather.3.cloned.1.call-start = ((), (), s32[]{:S(2)}) async-start(), calls=%async_computation.2 | async-start | bytes 1081344 | tf_op jit(solution)/shard_map/all_gather | solution.py:28
  90.0 510.5 %all-reduce.5.cloned.1.call-start = ((), (), s32[]{:S(2)}) async-start(), calls=%async_computation.3 | async-start | bytes 1048576 | tf_op jit(solution)/shard_map/psum | solution.py:58
  438.2 6.8 copy-start.1
  451.8 6.8 copy-start.1
  465.3 6.8 copy-start.1
  478.8 6.8 copy-start.1
  491.0 1.5 copy-start
  492.0 256.0 %reduce-scatter.2.cloned.1.call-start = ((), (), s32[]{:S(2)}) async-start(), calls=%async_computation.4 | async-start | bytes 2162688 | tf_op jit(solution)/shard_map/reduce_scatter | solution.py:59
Sparse Core Ops, SparseCore 0:
  89.4 285.8 all-reduce.2
  377.1 59.7 all-gather.2
  492.1 108.3 all-reduce.4
  603.6 144.3 reduce-scatter.1
where the time goes:
time: 757 us; the launch traced here: 756 us
  waiting for transfers between devices  593 us (78%)
  matrix products  48.6 us (6%)
  blocking collectives  44.9 us (6%)
  local copies, waits for them, and re-layouts  39.5 us (5%)
  between operations  13.8 us (2%)
  other arithmetic  13.3 us (2%)
    psum x1, waiting for transfers between devices, body(): centre_raw = lax.psum(picked, 'pts')  284 us
    reduce_scatter x1, waiting for transfers between devices, body(): lax.psum_scatter(centre_part, 'pts', scatter_dimension=1, tiled=True)  147 us
    psum x1, waiting for transfers between devices, body(): point_side = lax.psum(point_part, 'ctr')  108 us
    all_gather x1, waiting for transfers between devices, body(): panel_cols = lax.all_gather(right_cols, 'pts', axis=1, tiled=True)  53.1 us
    all_gather x1, blocking collectives, body(): indices = lax.all_gather(centre_index, 'pts', axis=0, tiled=True)  44.9 us
    gather x1, local copies, waits for them, and re-layouts, body(): taken_rows = jnp.take(points, jnp.clip(local_idx, 0, rows_here - 1), axis=1)  27.7 us
    dot_general x4, matrix products, tile_of(): lax.dot_general(scaled_blk, scaled_ctr, (((0,), (0,)), ((), ())), preferr...  27.1 us
  transfers between devices with their start and end apart: 4, of which 4 were waited for; matrix products, arithmetic and copies ran while one was open for 1% of the time, Pallas kernels for 0%

commit v1 on v0

v1 whole, which is shorter than its diff:
```python
import functools
import math

import jax
import jax.numpy as jnp
from jax import lax
from jax.experimental import pallas as pl
from jax.experimental.pallas import tpu as pltpu
from jax.sharding import PartitionSpec as P

F32, BF16, I32 = jnp.float32, jnp.bfloat16, jnp.int32
MESH = pl.DeviceIdType.MESH
LOG2E = math.log2(math.e)
FEAT = 90
ROWS = 96
COLS = 64
HERE = 2048
BLK = 256
GROUP = 32
PANELS = 8
SLOTS = 32
VMEM_LIMIT = 56 * 2**20


def pieces(value):
    first = value.astype(BF16).astype(F32)
    second = (value - first).astype(BF16).astype(F32)
    third = (value - first - second).astype(BF16).astype(F32)
    return first, second, third


def barrier_with(peers):
    barrier = pltpu.get_barrier_semaphore()
    total = 0
    for axis, count in peers:
        me = lax.axis_index(axis)

        def greet(step, _, axis=axis, count=count, me=me):
            pl.semaphore_signal(
                barrier, inc=1, device_id={axis: lax.rem(me + step, count)}, device_id_type=MESH
            )
            return 0

        lax.fori_loop(1, count, greet, 0)
        total += count - 1
    pl.semaphore_wait(barrier, total)


def gather_kernel(
    pts_ref, inv_ref, idx_ref, right_ref,
    block_ref, table_ref, flag_ref,
    idx_all, rank_all, cols_s, cols_l, lookup, rows_out, rows_in, flag_mine, flag_all,
    idx_send, idx_recv, row_send, row_recv, flag_send, flag_recv,
):
    me = lax.axis_index("pts")
    panel = lax.axis_index("ctr")
    barrier_with([("pts", GROUP), ("ctr", PANELS)])

    def idx_copy(step):
        return pltpu.make_async_remote_copy(
            src_ref=idx_ref, dst_ref=idx_all.at[me],
            send_sem=idx_send.at[step], recv_sem=idx_recv.at[me],
            device_id={"pts": lax.rem(me + step, GROUP)}, device_id_type=MESH,
        )

    def idx_arrival(step):
        source = lax.rem(me + step, GROUP)
        return pltpu.make_async_remote_copy(
            src_ref=idx_ref, dst_ref=idx_all.at[source],
            send_sem=idx_send.at[step], recv_sem=idx_recv.at[source],
            device_id={"pts": source}, device_id_type=MESH,
        )

    def send_idx(step, _):
        idx_copy(step).start()
        return 0

    lax.fori_loop(1, GROUP, send_idx, 0)
    idx_all[me] = idx_ref[...]

    scaled = (pts_ref[...] * inv_ref[...]).astype(BF16).astype(F32)
    half_norm = jnp.sum(scaled * scaled, axis=0, keepdims=True) * (-0.5 * LOG2E)
    first, second, third = pieces(half_norm)
    ones = jnp.ones((3, HERE), F32)
    cols_s[ROWS:, :] = jnp.zeros((128 - ROWS, HERE), F32)
    cols_l[ROWS:, :] = jnp.zeros((128 - ROWS, HERE), F32)
    cols_s[0:FEAT, :] = scaled
    cols_l[0:FEAT, :] = scaled * LOG2E
    cols_s[FEAT:FEAT + 3, :] = ones
    cols_l[FEAT + 3:ROWS, :] = ones
    for place, piece in enumerate((first, second, third)):
        cols_s[FEAT + 3 + place:FEAT + 4 + place, :] = piece
        cols_l[FEAT + place:FEAT + 1 + place, :] = piece
    for part in range(HERE // 128):
        span = slice(part * 128, (part + 1) * 128)
        high, low = part // 2, (part % 2) * 128
        lookup[low:low + 128, high * 128:(high + 1) * 128] = cols_s[:, span].T.astype(BF16)
        turned = cols_l[:, span].T
        upper = turned.astype(BF16)
        table_ref[span, 0:128] = upper
        table_ref[span, 128:256] = (turned - upper.astype(F32)).astype(BF16)

    before = (
        lax.broadcasted_iota(I32, (BLK, BLK), 0) < lax.broadcasted_iota(I32, (BLK, BLK), 1)
    ).astype(F32).astype(BF16)

    own_idx = idx_ref[...]
    own_owner = own_idx >> 11
    is_owner = lax.broadcasted_iota(I32, (GROUP, BLK), 0) == own_owner
    own_hits = jnp.where(is_owner, 1.0, 0.0)
    own_rank = jnp.dot(own_hits.astype(BF16), before, preferred_element_type=F32)
    own_rank = jnp.sum(own_rank * own_hits, axis=0, keepdims=True).astype(I32)
    own_slot = own_owner * SLOTS + own_rank

    def wait_idx(step, _):
        idx_arrival(step).wait_recv()
        return 0

    lax.fori_loop(1, GROUP, wait_idx, 0)

    idx_rows = jnp.concatenate([idx_all[d] for d in range(GROUP)], axis=0)
    owner = idx_rows >> 11
    hits = jnp.where(owner == me, 1.0, 0.0)
    rank = jnp.dot(hits.astype(BF16), before, preferred_element_type=F32)
    rank = jnp.where(hits > 0.5, rank, -1.0)
    for d in range(GROUP):
        rank_all[d] = rank[d:d + 1, :]

    slot_row = lax.broadcasted_iota(I32, (SLOTS, BLK), 0).astype(F32)
    low_col = lax.broadcasted_iota(I32, (SLOTS, BLK), 1)

    def row_copy(step):
        dest = lax.rem(me + step, GROUP)
        return pltpu.make_async_remote_copy(
            src_ref=rows_out.at[step], dst_ref=rows_in.at[me],
            send_sem=row_send.at[step], recv_sem=row_recv.at[me],
            device_id={"pts": dest}, device_id_type=MESH,
        )

    def row_arrival(step):
        source = lax.rem(me + step, GROUP)
        return pltpu.make_async_remote_copy(
            src_ref=rows_out.at[step], dst_ref=rows_in.at[source],
            send_sem=row_send.at[step], recv_sem=row_recv.at[source],
            device_id={"pts": source}, device_id_type=MESH,
        )

    per = 8

    def look_up(number, _):
        picks, highs = [], []
        for u in range(per):
            dest = lax.rem(me + number * per + u, GROUP)
            local = (idx_all[dest] & (HERE - 1)).astype(F32)
            chosen = rank_all[dest] == slot_row
            key = jnp.sum(jnp.where(chosen, local + 1.0, 0.0), axis=1, keepdims=True)
            key = key.astype(I32) - 1
            highs.append(key >> 8)
            picks.append(jnp.where((key & 255) == low_col, 1.0, 0.0).astype(BF16))
        pick = jnp.concatenate(picks, axis=0)
        high = jnp.concatenate(highs, axis=0)
        found = jnp.dot(pick, lookup[...], preferred_element_type=F32)
        rows = jnp.zeros((per * SLOTS, 128), F32)
        for h in range(8):
            rows = jnp.where(high == h, found[:, h * 128:(h + 1) * 128], rows)
        rows = rows.astype(BF16)
        for u in range(per):
            rows_out[number * per + u] = rows[u * SLOTS:(u + 1) * SLOTS, :]
        for u in range(per):
            step = number * per + u

            @pl.when(step > 0)
            def _():
                row_copy(step).start()

        return 0

    lax.fori_loop(0, GROUP // per, look_up, 0)
    rows_in[me] = rows_out[0]

    def count(source, most):
        here = jnp.sum(jnp.where(owner == source, 1.0, 0.0), axis=1, keepdims=True)
        return jnp.maximum(most, here)

    most = lax.fori_loop(0, GROUP, count, jnp.zeros((GROUP, 1), F32))
    flag_mine[...] = jnp.broadcast_to(jnp.max(most, axis=0, keepdims=True), (8, 128))

    def flag_copy(step):
        return pltpu.make_async_remote_copy(
            src_ref=flag_mine, dst_ref=flag_all.at[panel],
            send_sem=flag_send.at[step], recv_sem=flag_recv.at[panel],
            device_id={"ctr": lax.rem(panel + step, PANELS)}, device_id_type=MESH,
        )

    def flag_arrival(step):
        source = lax.rem(panel + step, PANELS)
        return pltpu.make_async_remote_copy(
            src_ref=flag_mine, dst_ref=flag_all.at[source],
            send_sem=flag_send.at[step], recv_sem=flag_recv.at[source],
            device_id={"ctr": source}, device_id_type=MESH,
        )

    def send_flag(step, _):
        flag_copy(step).start()
        return 0

    lax.fori_loop(1, PANELS, send_flag, 0)
    flag_all[panel] = flag_mine[...]

    place = jnp.where(
        lax.broadcasted_iota(I32, (GROUP * SLOTS, BLK), 0) == own_slot, 1.0, 0.0
    ).astype(BF16)

    def wait_rows(step, _):
        row_arrival(step).wait_recv()
        return 0

    lax.fori_loop(1, GROUP, wait_rows, 0)
    arrived = rows_in[...].reshape(GROUP * SLOTS, 128)
    centres = lax.dot_general(
        arrived, place, (((0,), (0,)), ((), ())), preferred_element_type=F32
    )
    block_ref[0:ROWS, :] = centres[0:ROWS, :].astype(BF16)
    block_ref[ROWS:ROWS + COLS, :] = right_ref[...]

    def wait_flags(step, _):
        flag_arrival(step).wait_recv()
        return 0

    lax.fori_loop(1, PANELS, wait_flags, 0)
    worst = flag_all[0]
    for c in range(1, PANELS):
        worst = jnp.maximum(worst, flag_all[c])
    flag_ref[...] = worst

    def drain(step, _):
        idx_copy(step).wait_send()
        row_copy(step).wait_send()
        return 0

    lax.fori_loop(1, GROUP, drain, 0)

    def drain_flags(step, _):
        flag_copy(step).wait_send()
        return 0

    lax.fori_loop(1, PANELS, drain_flags, 0)


def gather(points, inv_scale, centre_index, right_cols):
    vmem = pl.BlockSpec(memory_space=pltpu.VMEM)
    return pl.pallas_call(
        gather_kernel,
        out_shape=(
            jax.ShapeDtypeStruct((ROWS + COLS, BLK), BF16),
            jax.ShapeDtypeStruct((HERE, 256), BF16),
            jax.ShapeDtypeStruct((8, 128), F32),
        ),
        in_specs=[vmem] * 4,
        out_specs=[vmem] * 3,
        scratch_shapes=[
            pltpu.VMEM((GROUP, 1, BLK), I32),
            pltpu.VMEM((GROUP, 1, BLK), F32),
            pltpu.VMEM((128, HERE), F32),
            pltpu.VMEM((128, HERE), F32),
            pltpu.VMEM((256, 1024), BF16),
            pltpu.VMEM((GROUP, SLOTS, 128), BF16),
            pltpu.VMEM((GROUP, SLOTS, 128), BF16),
            pltpu.VMEM((8, 128), F32),
            pltpu.VMEM((PANELS, 8, 128), F32),
            pltpu.SemaphoreType.DMA((GROUP,)),
            pltpu.SemaphoreType.DMA((GROUP,)),
            pltpu.SemaphoreType.DMA((GROUP,)),
            pltpu.SemaphoreType.DMA((GROUP,)),
            pltpu.SemaphoreType.DMA((PANELS,)),
            pltpu.SemaphoreType.DMA((PANELS,)),
        ],
        compiler_params=pltpu.CompilerParams(
            collective_id=0, has_side_effects=True, vmem_limit_bytes=VMEM_LIMIT
        ),
        name="gather_centres",
    )(points, inv_scale[:, None], centre_index[None, :], right_cols)


def dense_block(points, centre_index, inv_scale, right_cols):
    offset = lax.axis_index("pts") * HERE
    indices = lax.all_gather(centre_index, "pts", axis=0, tiled=True)
    local = indices - offset
    inside = (local >= 0) & (local < HERE)
    taken = jnp.take(points, jnp.clip(local, 0, HERE - 1), axis=1)
    picked = jnp.where(inside[None, :], taken, 0.0)
    raw = lax.psum_scatter(picked, "pts", scatter_dimension=1, tiled=True)
    scaled = lax.reduce_precision(raw * inv_scale[:, None], 8, 7)
    half_norm = jnp.sum(scaled * scaled, axis=0, keepdims=True) * (-0.5 * LOG2E)
    first = lax.reduce_precision(half_norm, 8, 7)
    second = lax.reduce_precision(half_norm - first, 8, 7)
    third = lax.reduce_precision(half_norm - first - second, 8, 7)
    rows = jnp.concatenate([scaled, jnp.ones((3, BLK), F32), first, second, third], axis=0)
    return jnp.concatenate([rows.astype(BF16), right_cols], axis=0)


CHIPS = 16
TILE_I = 1024


def product_kernel(
    block_ref, table_ref, left_ref,
    point_ref, centre_ref,
    blocks, point_acc, mine, for_pair, from_pair, to_home, at_home,
    x_out, x_in, z_out, z_in, back_out, back_in,
    rail_send, pair_send, block_recv, part_send, part_recv, home_send, home_recv,
    x_send, x_recv, z_send, z_recv, back_send, back_recv,
):
    me = lax.axis_index("pts")
    panel = lax.axis_index("ctr")
    z, y, core = me // 8, lax.rem(me // 2, 4), lax.rem(me, 2)
    x, z_hi = panel // 2, lax.rem(panel, 2)

    def at(dz, dy, c):
        return lax.rem(z + dz, 4) * 8 + lax.rem(y + dy, 4) * 2 + c

    def before(dz, dy, c):
        return lax.rem(z + 4 - dz, 4) * 8 + lax.rem(y + 4 - dy, 4) * 2 + c

    other = 1 - core
    pair = {"pts": at(0, 0, other)}
    cross = {"ctr": x * 2 + 1 - z_hi}

    barrier = pltpu.get_barrier_semaphore()

    def greet(m, _):
        pl.semaphore_signal(
            barrier, inc=1, device_id={"pts": at(lax.rem(m, 4), m // 4, core)}, device_id_type=MESH
        )
        return 0

    lax.fori_loop(1, CHIPS, greet, 0)
    pl.semaphore_signal(barrier, inc=1, device_id=pair, device_id_type=MESH)
    pl.semaphore_signal(barrier, inc=1, device_id=cross, device_id_type=MESH)
    for dx in (1, 2, 3):
        pl.semaphore_signal(
            barrier, inc=1, device_id={"ctr": lax.rem(x + dx, 4) * 2 + z_hi}, device_id_type=MESH
        )
    pl.semaphore_wait(barrier, CHIPS - 1 + 5)

    def rail_copy(slot, dz, dy, number):
        return pltpu.make_async_remote_copy(
            src_ref=blocks.at[slot], dst_ref=blocks.at[slot],
            send_sem=rail_send.at[number], recv_sem=block_recv.at[slot],
            device_id={"pts": at(dz, dy, core)}, device_id_type=MESH,
        )

    def pair_copy(slot, m):
        return pltpu.make_async_remote_copy(
            src_ref=blocks.at[slot], dst_ref=blocks.at[slot],
            send_sem=pair_send.at[m], recv_sem=block_recv.at[slot],
            device_id=pair, device_id_type=MESH,
        )

    def pass_on(slot, dz):
        for dy in (1, 2, 3):
            rail_copy(slot, 0, dy, 3 + dz * 3 + dy - 1).start()

    own = at(0, 0, core)
    blocks[own] = block_ref[...]
    pair_copy(own, 0).start()
    for dz in (1, 2, 3):
        rail_copy(own, dz, 0, dz - 1).start()
    pass_on(own, 0)
    point_acc[...] = jnp.zeros_like(point_acc)

    def part_copy(m):
        return pltpu.make_async_remote_copy(
            src_ref=for_pair.at[m], dst_ref=from_pair.at[m],
            send_sem=part_send.at[m], recv_sem=part_recv.at[m],
            device_id=pair, device_id_type=MESH,
        )

    def home_copy(m):
        return pltpu.make_async_remote_copy(
            src_ref=to_home.at[m], dst_ref=at_home.at[m],
            send_sem=home_send.at[m], recv_sem=home_recv.at[m],
            device_id={"pts": at(lax.rem(m, 4), m // 4, core)}, device_id_type=MESH,
        )

    def finish(m):
        part_copy(m).wait_recv()
        to_home[m] = (mine[m] + from_pair[m].astype(F32)).astype(BF16)

    def advance(m, _):
        ahead = m + 1

        @pl.when(ahead < CHIPS)
        def _():
            dz, dy = lax.rem(ahead, 4), ahead // 4
            slot = at(dz, dy, core)
            rail_copy(slot, 0, 0, 0).wait_recv()
            pair_copy(slot, ahead).start()

            @pl.when(ahead < 4)
            def _():
                pass_on(slot, ahead)

        dz, dy = lax.rem(m, 4), m // 4
        slot, pair_slot = at(dz, dy, core), at(dz, dy, other)
        pair_copy(pair_slot, m).wait_recv()

        blank = jnp.zeros((128 - ROWS, BLK), BF16)
        sides, rights = [], []
        for s in (slot, pair_slot):
            cut = blocks[s, 0:ROWS, :]
            sides.append(jnp.concatenate([cut, blank, cut, blank], axis=0))
            rights.append(blocks[s, ROWS:ROWS + COLS, :])
        side = jnp.concatenate(sides, axis=1)
        right = jnp.concatenate(rights, axis=1)
        total = None
        for t in range(HERE // TILE_I):
            span = slice(t * TILE_I, (t + 1) * TILE_I)
            power = jnp.dot(table_ref[span, :], side, preferred_element_type=F32)
            kernel = jnp.exp2(jnp.minimum(power, 0.0)).astype(BF16)
            point_acc[:, span] += lax.dot_general(
                right, kernel, (((1,), (1,)), ((), ())), preferred_element_type=F32
            )
            part = jnp.dot(left_ref[:, span], kernel, preferred_element_type=F32)
            total = part if total is None else total + part
        mine[m] = total[:, 0:BLK]
        for_pair[m] = total[:, BLK:].astype(BF16)
        part_copy(m).start()

        @pl.when(m > 1)
        def _():
            finish(m - 1)
            home_copy(m - 1).start()

        @pl.when(m == 1)
        def _():
            finish(0)

        return 0

    lax.fori_loop(0, CHIPS, advance, 0)

    part = HERE // 4

    def x_copy(dx):
        return pltpu.make_async_remote_copy(
            src_ref=x_out.at[dx - 1], dst_ref=x_in.at[dx - 1],
            send_sem=x_send.at[dx - 1], recv_sem=x_recv.at[dx - 1],
            device_id={"ctr": lax.rem(x + dx, 4) * 2 + z_hi}, device_id_type=MESH,
        )

    def own_part(step):
        return pl.ds(pl.multiple_of(lax.rem(x + step, 4) * part, part), part)

    for dx in (1, 2, 3):
        x_out[dx - 1] = point_acc[:, own_part(dx)].astype(BF16)
        x_copy(dx).start()

    finish(CHIPS - 1)
    home_copy(CHIPS - 1).start()

    total = point_acc[:, own_part(0)]
    for dx in (1, 2, 3):
        x_copy(dx).wait_recv()
        total = total + x_in[dx - 1].astype(F32)
    z_out[...] = total.astype(BF16)
    z_copy = pltpu.make_async_remote_copy(
        src_ref=z_out, dst_ref=z_in, send_sem=z_send, recv_sem=z_recv,
        device_id=cross, device_id_type=MESH,
    )
    z_copy.start()

    def wait_home(m, _):
        home_copy(m).wait_recv()
        return 0

    z_copy.wait_recv()
    back_out[...] = (z_out[...].astype(F32) + z_in[...].astype(F32)).astype(BF16)

    def back_copy(dx):
        return pltpu.make_async_remote_copy(
            src_ref=back_out, dst_ref=back_in.at[dx - 1],
            send_sem=back_send.at[dx - 1], recv_sem=back_recv.at[dx - 1],
            device_id={"ctr": lax.rem(x + dx, 4) * 2 + z_hi}, device_id_type=MESH,
        )

    for dx in (1, 2, 3):
        back_copy(dx).start()
    point_ref[:, own_part(0)] = back_out[...].astype(F32)

    lax.fori_loop(1, CHIPS, wait_home, 0)
    centre = to_home[0].astype(F32)
    for m in range(1, CHIPS):
        centre = centre + at_home[m].astype(F32)
    centre_ref[...] = centre

    for dx in (1, 2, 3):
        back_copy(dx).wait_recv()
        point_ref[:, own_part(4 - dx)] = back_in[dx - 1].astype(F32)

    for number in range(15):
        rail_copy(own, 0, 0, number).wait_send()
    for dx in (1, 2, 3):
        x_copy(dx).wait_send()
        back_copy(dx).wait_send()
    z_copy.wait_send()

    def drain(m, _):
        pair_copy(own, m).wait_send()
        part_copy(m).wait_send()
        return 0

    lax.fori_loop(0, CHIPS, drain, 0)

    def drain_home(m, _):
        home_copy(m).wait_send()
        return 0

    lax.fori_loop(1, CHIPS, drain_home, 0)


def products(block, table, left_cols):
    vmem = pl.BlockSpec(memory_space=pltpu.VMEM)
    dma = pltpu.SemaphoreType.DMA
    part = HERE // 4
    return pl.pallas_call(
        product_kernel,
        out_shape=(
            jax.ShapeDtypeStruct((COLS, HERE), F32),
            jax.ShapeDtypeStruct((COLS, BLK), F32),
        ),
        in_specs=[vmem] * 3,
        out_specs=[vmem] * 2,
        scratch_shapes=[
            pltpu.VMEM((GROUP, ROWS + COLS, BLK), BF16),
            pltpu.VMEM((COLS, HERE), F32),
            pltpu.VMEM((CHIPS, COLS, BLK), F32),
            pltpu.VMEM((CHIPS, COLS, BLK), BF16),
            pltpu.VMEM((CHIPS, COLS, BLK), BF16),
            pltpu.VMEM((CHIPS, COLS, BLK), BF16),
            pltpu.VMEM((CHIPS, COLS, BLK), BF16),
            pltpu.VMEM((3, COLS, part), BF16),
            pltpu.VMEM((3, COLS, part), BF16),
            pltpu.VMEM((COLS, part), BF16),
            pltpu.VMEM((COLS, part), BF16),
            pltpu.VMEM((COLS, part), BF16),
            pltpu.VMEM((3, COLS, part), BF16),
            dma((15,)), dma((CHIPS,)), dma((GROUP,)), dma((CHIPS,)), dma((CHIPS,)),
            dma((CHIPS,)), dma((CHIPS,)),
            dma((3,)), dma((3,)), dma, dma, dma((3,)), dma((3,)),
        ],
        compiler_params=pltpu.CompilerParams(
            collective_id=1, has_side_effects=True, vmem_limit_bytes=VMEM_LIMIT
        ),
        name="kernel_products",
    )(block, table, left_cols)


def body(points, centre_index, inv_scale, left_cols, right_cols):
    block, table, flag = gather(points, inv_scale, centre_index, right_cols)
    block = lax.cond(
        flag[0, 0] > SLOTS,
        lambda: dense_block(points, centre_index, inv_scale, right_cols),
        lambda: block,
    )
    return products(block, table, left_cols)


def solution(mesh):
    return jax.shard_map(
        body,
        mesh=mesh,
        in_specs=(P(None, "pts"), P(("ctr", "pts")), P(), P(None, "pts"), P(None, ("ctr", "pts"))),
        out_specs=(P(None, "pts"), P(None, ("ctr", "pts"))),
        check_vma=False,
    )
```

time: 757 us -> 108 us (0.14)
  waiting for transfers between devices: 593 us -> 0 us
  Pallas kernels: 0 us -> 86.2 us
  matrix products: 48.6 us -> 0 us
  blocking collectives: 44.9 us -> 0 us
  local copies, waits for them, and re-layouts: 39.5 us -> 5.92 us
  other arithmetic: 13.3 us -> 0 us
    psum x2 -> x0, waiting for transfers between devices: 392 us -> none  [the longest x1 284 us: body(): centre_raw = lax.psum(picked, 'pts')]
    reduce_scatter x1 -> x0, waiting for transfers between devices: 147 us -> none  [body(): lax.psum_scatter(centre_part, 'pts', scatter_dimension=1, tiled=True)]
    pallas_call x0 -> x2, Pallas kernels: none -> 86.2 us  [the longest x1 58.3 us: products(): pl.pallas_call(product_kernel, out_shape=(jax.ShapeDtypeStruct((COLS, HER...]
    all_gather x1 -> x0, waiting for transfers between devices: 53.1 us -> none  [body(): panel_cols = lax.all_gather(right_cols, 'pts', axis=1, tiled=True)]
    dot_general x12 -> x0, matrix products: 48.6 us -> none  [the longest x4 27.1 us: tile_of(): lax.dot_general(scaled_blk, scaled_ctr, (((0,), (0,)), ((), ())), preferr...]
    all_gather x1 -> x0, blocking collectives: 44.9 us -> none  [body(): indices = lax.all_gather(centre_index, 'pts', axis=0, tiled=True)]
    gather x1 -> x0, local copies, waits for them, and re-layouts: 27.7 us -> none  [body(): taken_rows = jnp.take(points, jnp.clip(local_idx, 0, rows_here - 1), axis=1)]
    select_n x1 -> x0, other arithmetic: 7.64 us -> none  [body(): picked = jnp.where(inside[None, :], taken_rows, 0.0)]
  transfers between devices with their start and end apart: 4 -> 0, of which waited for: 4 -> 0; matrix products, arithmetic and copies ran while one was open for 1% -> 0% of each run, Pallas kernels for 0% -> 0%
where the time goes in v1:
time: 108 us; the launch traced here: 107 us
  Pallas kernels  86.2 us (80%)
  between operations  14.7 us (14%)
  local copies, waits for them, and re-layouts  5.92 us (5%)
    pallas_call x1, Pallas kernels, products(): pl.pallas_call(product_kernel, out_shape=(jax.ShapeDtypeStruct((COLS, HER...  58.3 us
    pallas_call x1, Pallas kernels, gather(): pl.pallas_call(gather_kernel, out_shape=(jax.ShapeDtypeStruct((ROWS + COL...  27.9 us
    unnamed x2, local copies, waits for them, and re-layouts  3.34 us

profile of v1, /device:TPU:4, one launch (start us, length us, event | category | flops | bytes accessed | tf_op | source)
XLA Modules:
  0.0 106.9 jit_solution(10343132247312305576)
XLA Ops:
  7.2 1.4 %copy.29.inv_ref = f32[90,1]{1,0:T(8,128)} copy(f32[90,1]{0,1:T(1,128)} %bitcast.13) | data formatting | bytes 720 | tf_op jit(solution)/shard_map/broadcast_in_dim | solution.py:282
  8.5 27.9 %gather_centres.1 = (bf16[160,256]{1,0:T(8,128)(2,1)S(1)}, bf16[2048,256]{1,0:T(8,128)(2,1)}, f32[8,128]{1,0:T(8,128)}) custom-call(f32[90,2048]{1,0:T(8,128)} %pts_ref.1, f32[90,1]{1,0:T(8,128)} %copy.29.inv_ref, s32[1,256]{1,0:T(1,128)} %bitcast.10, bf16[64,256]{1,0:T(8,128)(2,1)} %right_ref.1), custom_call_target="tpu_custom_call" | custom-call | tf_op jit(solution)/shard_map/gather_centres/pallas_call | solution.py:252
  36.5 1.2 %slice.3 = f32[1,1]{1,0:T(1,128)} slice(f32[8,128]{1,0:T(8,128)} %get-tuple-element.21), slice={[0:1], [0:1]} | slice | bytes 8 | tf_op jit(solution)/shard_map/slice | solution.py:562
  38.3 58.3 %kernel_products.1 = (f32[64,2048]{1,0:T(8,128)}, f32[64,256]{1,0:T(8,128)}) custom-call(bf16[160,256]{1,0:T(8,128)(2,1)S(1)} %get-tuple-element.40.block_ref, bf16[2048,256]{1,0:T(8,128)(2,1)} %get-tuple-element.23.table_ref, bf16[64,2048]{1,0:T(8,128)(2,1)} %left_ref.1), custom_call_target="tpu_custom_call" | custom-call | tf_op jit(solution)/shard_map/kernel_products/pallas_call | solution.py:526
  96.7 1.9 %copy.40 = f32[64,2048]{1,0:T(8,128)} copy(f32[64,2048]{1,0:T(8,128)} %get-tuple-element.50) | data formatting | bytes 1048576
  98.5 1.5 %copy.41 = f32[64,256]{1,0:T(8,128)} copy(f32[64,256]{1,0:T(8,128)} %get-tuple-element.51) | data formatting | bytes 131072
  (1 shorter events, 0.0 us)
